TPU v7x, 32 devices: a whole 2x2x4 slice. The times are simulated.
32 devices in a mesh: groups: 2 (over x), adapter: 4 (over y, core), tensor: 4 (over z).
Axes of the slice: x: 2, y: 2, z: 4, core: 2. Of those that a mesh axis runs over, the one named last changes fastest.
Arguments:
- tokens: bfloat16 [8192, 8192], P(('groups', 'adapter'), 'tensor'), parts along dimension 0, may hold values from -6 to 6
- shared_weight: bfloat16 [8192, 2048], P('tensor'), may hold values from -0.0625 to 0.0625
- adapter_down_weight: bfloat16 [8192, 2048], P('tensor', 'adapter'), may hold values from -0.0625 to 0.0625
- adapter_up_weight: bfloat16 [2048, 2048], P('adapter', 'tensor'), may hold values from -0.75 to 0.75
- row_adapter_index: int32 [8192], P(('groups', 'adapter')), parts along dimension 0, may hold values from 0 to 31, as said below
Outputs:
- projected: bfloat16 [8192, 2048], P(('groups', 'adapter'), 'tensor'), parts along dimension 0
There are 2 independent parts, one for each index of `groups`. A program takes and returns all parts, laid end to end along the dimension named above; an argument that names none is the same for every part. Nothing has to cross between parts.
Inputs may be any that keep to these rules, and one draw needn't show every extreme that they name: `row_adapter_index`: adapter a is held by the device of index a // 8 along adapter. In every device's block of 1024 rows the rows go to the holders in the same numbers: one holder, the same for the whole part, has exactly 320 of them, and the others share the rest as evenly as possible, so that each has at most 235.
All inputs are finite; a program needn't handle non-finite values.
Results may differ from a plain program's by a relative error of at most 0.014.
Values may be sent and summed in bfloat16 or wider, within the bound.
A program may use at most 128 MiB of HBM per device.

v0:
```python
import jax
import jax.numpy as jnp
from jax import lax
from jax.sharding import PartitionSpec as P

AD_DEV = 8


def pick_adapter(rank_products, adapter_selector):
    count = rank_products.shape[0]
    return jnp.sum(
        rank_products.reshape(count, adapter_selector.shape[1], -1) * adapter_selector[:, :, None],
        axis=1,
    )


def expanded_rank(reduced_rows, adapter_selector):
    count = reduced_rows.shape[0]
    widened = adapter_selector.astype(jnp.bfloat16)[:, :, None] * reduced_rows[:, None, :]
    return widened.reshape(count, -1)


def pack_rows(tokens, holder, local_index, taken, capacity, holders):
    hits = (
        (holder[:, None] == jnp.arange(holders, dtype=jnp.int32)[None, :]) & taken[:, None]
    ).astype(jnp.int32)
    position = jnp.sum((jnp.cumsum(hits, axis=0) - 1) * hits, axis=1)
    slot_index = jnp.where(taken, holder * capacity + position, holders * capacity)
    width = tokens.shape[1]
    gathered_rows = (
        jnp.zeros((holders * capacity + 1, width), jnp.bfloat16).at[slot_index].set(tokens)
    )
    gathered_index = (
        jnp.full((holders * capacity + 1,), -1.0, jnp.bfloat16)
        .at[slot_index]
        .set(local_index.astype(jnp.bfloat16))
    )
    return (
        gathered_rows[:-1].reshape(holders, capacity, width),
        gathered_index[:-1].reshape(holders, capacity),
        slot_index,
    )


def foreign_rows(gathered_rows, gathered_index, adapter_down_weight, adapter_up_weight):
    rows_in = lax.all_to_all(gathered_rows, "adapter", split_axis=0, concat_axis=0, tiled=True)
    index_in = lax.all_to_all(gathered_index, "adapter", split_axis=0, concat_axis=0, tiled=True)
    sources, count = index_in.shape
    flattened_rows = rows_in.reshape(sources * count, rows_in.shape[2])
    flat_index = index_in.reshape(-1).astype(jnp.int32)
    adapter_selector = (flat_index[:, None] == jnp.arange(AD_DEV, dtype=jnp.int32)[None, :]).astype(
        jnp.float32
    )
    rank_products = jnp.dot(flattened_rows, adapter_down_weight, preferred_element_type=jnp.float32)
    partial_value = pick_adapter(rank_products, adapter_selector)
    reduced_rows = lax.psum(partial_value.astype(jnp.bfloat16), "tensor")
    delta_rows = jnp.dot(
        expanded_rank(reduced_rows, adapter_selector),
        adapter_up_weight,
        preferred_element_type=jnp.float32,
    ).astype(jnp.bfloat16)
    delta_rows = delta_rows.reshape(sources, count, delta_rows.shape[1])
    return lax.all_to_all(delta_rows, "adapter", split_axis=0, concat_axis=0, tiled=True)


def unpack_rows(delivered_output, slot_index):
    flat = delivered_output.reshape(-1, delivered_output.shape[2])
    padded = jnp.concatenate([flat, jnp.zeros((1, flat.shape[1]), jnp.bfloat16)], axis=0)
    return padded[slot_index]


def per_device(tokens, shared_weight, adapter_down_weight, adapter_up_weight, row_adapter_index):
    holders = lax.axis_size("adapter")
    row_count = tokens.shape[0]
    capacity = 5 * row_count // 16
    holder = row_adapter_index // AD_DEV
    local_index = row_adapter_index % AD_DEV
    base_partial = jnp.dot(tokens, shared_weight, preferred_element_type=jnp.float32)
    base_total = lax.psum_scatter(
        base_partial.astype(jnp.bfloat16), "tensor", scatter_dimension=1, tiled=True
    ).astype(jnp.float32)
    taken = jnp.ones((row_count,), jnp.bool_)
    gathered_rows, gathered_index, slot_index = pack_rows(
        tokens, holder, local_index, taken, capacity, holders
    )
    delivered_output = foreign_rows(
        gathered_rows, gathered_index, adapter_down_weight, adapter_up_weight
    )
    delta_rows = unpack_rows(delivered_output, slot_index).astype(jnp.float32)
    return (base_total + delta_rows).astype(jnp.bfloat16)


def solution(mesh):
    in_specs = (
        P(("groups", "adapter"), "tensor"),
        P("tensor", None),
        P("tensor", "adapter"),
        P("adapter", "tensor"),
        P(("groups", "adapter")),
    )
    out_specs = P(("groups", "adapter"), "tensor")
    return jax.shard_map(
        per_device, mesh=mesh, in_specs=in_specs, out_specs=out_specs, check_vma=False
    )
```

profile of v0, /device:TPU:0, one launch (start us, length us, event | category | flops | bytes accessed | tf_op | source)
XLA Modules:
  0.0 234.4 jit_solution(1559214421437808493)
XLA Ops:
  6.5 0.0 copy-start
  6.5 0.8 fusion.8
  7.3 1.1 reduce-window.6
  8.4 0.2 slice_reduce_fusion
  8.7 0.2 reduce-window.9
  8.8 0.1 add_bitcast_fusion
  9.0 7.6 %scatter_custom_fusion = bf16[1281]{0:T(1024)(128)(2,1)S(1)} fusion(s32[1024]{0:T(1024)S(1)} %get-tuple-element.6, bf16[1024]{0:T(1024)(128)(2,1)S(1)} %get-tuple-element.9, bf16[]{:T(256)} %constant.38.clone.1), kind=kCustom, calls=%fused_computation.34 | custom fusion | bytes 2564 | tf_op jit(solution)/shard_map/scatter | solution.py:36
  16.6 0.1 all_to_all.16
  16.7 0.5 broadcast.91
  17.2 0.7 reduce.4
  17.8 0.7 reshape.130
  18.5 4.2 %all-to-all-start = ((bf16[4,2,160]{2,1,0:T(2,128)(2,1)}), bf16[4,2,160]{2,1,0:T(2,128)(2,1)S(1)}, u32[]{:S(2)}, u32[]{:S(2)}) async-start(bf16[4,2,160]{2,1,0:T(2,128)(2,1)} %reshape.130), calls=%async_computation.1 | async-start | bytes 8192 | tf_op jit(solution)/shard_map/all_to_all | solution.py:47
  22.8 10.7 %scatter_custom_fusion.1 = bf16[1281,2048]{1,0:T(8,128)(2,1)} fusion(s32[1024]{0:T(1024)S(1)} %get-tuple-element.6, bf16[1024,2048]{1,0:T(8,128)(2,1)} %param.5, bf16[]{:T(256)} %constant.47.clone.1), kind=kCustom, calls=%fused_computation.6 | custom fusion | bytes 5247488 | tf_op jit(solution)/shard_map/scatter | solution.py:31
  33.5 5.7 %slice.20 = bf16[1280,2048]{1,0:T(8,128)(2,1)} slice(bf16[1281,2048]{1,0:T(8,128)(2,1)} %scatter_custom_fusion.1), slice={[0:1280], [0:2048]} | slice | bytes 10485760 | tf_op jit(solution)/shard_map/slice | solution.py:39
  39.1 0.0 all-to-all-done
  39.1 0.0 copy-start.1
  39.1 5.2 %all-to-all-start.1 = ((bf16[4,320,2048]{2,1,0:T(8,128)(2,1)}), bf16[4,320,2048]{2,1,0:T(8,128)(2,1)}, u32[]{:S(2)}, u32[]{:S(2)}) async-start(bf16[4,320,2048]{2,1,0:T(8,128)(2,1)} %bitcast.33), calls=%async_computation.2 | async-start | bytes 10485760 | tf_op jit(solution)/shard_map/all_to_all | solution.py:46
  44.3 0.2 all-reduce.3.cloned.1.call-start
  44.6 0.0 copy-done.1
  44.6 2.4 %copy.10 = bf16[2048,512]{0,1:T(8,128)(2,1)} copy(bf16[2048,512]{1,0:T(8,128)(2,1)S(1)} %copy-done.1) | data formatting | bytes 4194304 | tf_op args[2]
  47.0 0.1 reshape.131
  47.1 0.1 reshape.95
  47.2 56.6 %all-to-all-done.1 = bf16[4,320,2048]{2,1,0:T(8,128)(2,1)} async-done(((bf16[4,320,2048]{2,1,0:T(8,128)(2,1)}), bf16[4,320,2048]{2,1,0:T(8,128)(2,1)}, u32[]{:S(2)}, u32[]{:S(2)}) %all-to-all-start.1) | async-done | bytes 5242912 | tf_op jit(solution)/shard_map/all_to_all | solution.py:46
  103.8 6.8 %fusion.2 = bf16[1280,64]{0,1:T(8,128)(2,1)} fusion(bf16[1280,2048,1]{1,0,2:T(8,128)(2,1)} %bitcast.4, bf16[8,64,2048]{2,1,0:T(8,128)(2,1)} %bitcast.35, f32[1280,8]{0,1:T(8,128)S(1)} %get-tuple-element.8), kind=kOutput, calls=%fused_computation.9 | convolution fusion | flops 2685583360 | bytes 7544832 | tf_op jit(solution)/shard_map/dot_general | solution.py:54
  110.6 0.0 all-reduce.3.cloned.1.call-update
  110.6 0.0 reduce-scatter.2.cloned.1.call-start
  110.7 13.8 %convolution_convert_fusion = bf16[1024,2048]{1,0:T(8,128)(2,1)} fusion(bf16[1024,2048]{1,0:T(8,128)(2,1)} %param.5, bf16[2048,2048]{1,0:T(8,128)(2,1)} %param.6), kind=kOutput, calls=%fused_computation.3 | convolution fusion | flops 8592031744 | bytes 16777216 | tf_op jit(solution)/shard_map/dot_general | solution.py:78
  124.5 0.0 reduce-scatter.2.cloned.1.call-update
  124.5 21.7 %all-reduce.3.cloned.1.call-done = bf16[1280,64]{0,1:T(8,128)(2,1)} async-done(((bf16[1280,64]{0,1:T(8,128)(2,1)}), bf16[1280,64]{0,1:T(8,128)(2,1)}) %all-reduce.3.cloned.1.call-update) | async-done | bytes 163856 | tf_op jit(solution)/shard_map/psum | solution.py:56
  146.2 1.0 broadcast_multiply_fusion
  147.2 0.0 copy-done
  147.2 0.9 convolution_convert_fusion.1
  148.1 19.8 %all_to_all.20 = bf16[4,320,512]{2,1,0:T(8,128)(2,1)S(1)} all-to-all(bf16[4,320,512]{2,1,0:T(8,128)(2,1)S(1)} %bitcast.37), channel_id=1, replica_groups=mesh['groups'=2,'adapter'=4,'tensor'=4] {'adapter'}, dimensions={0} | all-to-all | bytes 2621440 | tf_op jit(solution)/shard_map/all_to_all | solution.py:63
  167.9 0.1 concatenate.3
  168.0 4.0 %gather_fusion = bf16[1024,512]{1,0:T(8,128)(2,1)S(1)} fusion(bf16[1281,512]{1,0:T(8,128)(2,1)S(1)} %concatenate.3, s32[1024]{0:T(1024)S(1)} %get-tuple-element.5), kind=kCustom, calls=%fused_computation | custom fusion | bytes 2101248 | tf_op jit(solution)/shard_map/gather | solution.py:69
  172.0 53.1 %reduce-scatter.2.cloned.1.call-done = bf16[1024,512]{1,0:T(8,128)(2,1)} async-done(((bf16[1024,2048]{1,0:T(8,128)(2,1)}), bf16[1024,512]{1,0:T(8,128)(2,1)}) %reduce-scatter.2.cloned.1.call-update) | async-done | bytes 1048592 | tf_op jit(solution)/shard_map/reduce_scatter | solution.py:79
  225.1 2.5 %add_convert_fusion = bf16[1024,512]{1,0:T(8,128)(2,1)} fusion(bf16[1024,512]{1,0:T(8,128)(2,1)S(1)} %gather_fusion, bf16[1024,512]{1,0:T(8,128)(2,1)} %reduce-scatter.2.cloned.1.call-done), kind=kLoop, calls=%fused_computation.8 | loop fusion | flops 2097152 | bytes 3145728 | tf_op jit(solution)/shard_map/convert_element_type | solution.py:90
  (5 shorter events, 0.1 us)
Async XLA Ops:
  6.5 140.7 %copy-start = (bf16[512,512]{1,0:T(8,128)(2,1)S(1)}, bf16[512,512]{1,0:T(8,128)(2,1)}, u32[]{:S(2)}) copy-start(bf16[512,512]{1,0:T(8,128)(2,1)} %param.8) | copy-start | bytes 1572868
  18.5 20.6 %all-to-all-start = ((bf16[4,2,160]{2,1,0:T(2,128)(2,1)}), bf16[4,2,160]{2,1,0:T(2,128)(2,1)S(1)}, u32[]{:S(2)}, u32[]{:S(2)}) async-start(bf16[4,2,160]{2,1,0:T(2,128)(2,1)} %reshape.130), calls=%async_computation.1 | async-start | bytes 8192 | tf_op jit(solution)/shard_map/all_to_all | solution.py:47
  39.1 5.4 %copy-start.1 = (bf16[2048,512]{1,0:T(8,128)(2,1)S(1)}, bf16[2048,512]{1,0:T(8,128)(2,1)}, u32[]{:S(2)}) copy-start(bf16[2048,512]{1,0:T(8,128)(2,1)} %param.7) | copy-start | bytes 6291460
  39.1 64.7 %all-to-all-start.1 = ((bf16[4,320,2048]{2,1,0:T(8,128)(2,1)}), bf16[4,320,2048]{2,1,0:T(8,128)(2,1)}, u32[]{:S(2)}, u32[]{:S(2)}) async-start(bf16[4,320,2048]{2,1,0:T(8,128)(2,1)} %bitcast.33), calls=%async_computation.2 | async-start | bytes 10485760 | tf_op jit(solution)/shard_map/all_to_all | solution.py:46
  44.3 101.9 %all-reduce.3.cloned.1.call-start = ((), (), s32[]{:S(2)}) async-start(), calls=%async_computation.5 | async-start | bytes 327680 | tf_op jit(solution)/shard_map/psum | solution.py:56
  110.6 114.5 %reduce-scatter.2.cloned.1.call-start = ((), (), s32[]{:S(2)}) async-start(), calls=%async_computation.4 | async-start | bytes 5242880 | tf_op jit(solution)/shard_map/reduce_scatter | solution.py:79
Sparse Core Ops, SparseCore 0:
  110.7 35.4 all-reduce.2
  148.6 76.4 reduce-scatter.1
where the time goes:
time: 235 us; the launch traced here: 234 us
  waiting for transfers between devices  131 us (56%)
  local copies, waits for them, and re-layouts  32.1 us (14%)
  matrix products  21.5 us (9%)
  blocking collectives  19.8 us (8%)
  between operations  13.5 us (6%)
  starting transfers between devices  9.71 us (4%)
  other arithmetic  6.4 us (3%)
    all_to_all x1, waiting for transfers between devices, foreign_rows(): lax.all_to_all(gathered_rows, 'adapter', split_axis=0, concat_axis=0, til...  56.6 us
    reduce_scatter x1, waiting for transfers between devices, per_device(): lax.psum_scatter(base_partial.astype(jnp.bfloat16), 'tensor', scatter_dim...  53.1 us
    psum x1, waiting for transfers between devices, foreign_rows(): reduced_rows = lax.psum(partial_value.astype(jnp.bfloat16), 'tensor')  21.7 us
    all_to_all x1, blocking collectives, foreign_rows(): lax.all_to_all(delta_rows, 'adapter', split_axis=0, concat_axis=0, tiled=...  19.8 us
    dot_general x1, matrix products, per_device(): jnp.dot(tokens, shared_weight, preferred_element_type=jnp.float32)  13.8 us
    scatter x1, local copies, waits for them, and re-layouts, pack_rows(): jnp.zeros((holders * capacity + 1, width), jnp.bfloat16).at[slot_index]  10.7 us
    scatter x1, local copies, waits for them, and re-layouts, pack_rows(): gathered_index = jnp.full((holders * capacity + 1,), -1.0, jnp.bfloat16)....  7.59 us
    dot_general x1, matrix products, foreign_rows(): jnp.dot(flattened_rows, adapter_down_weight, preferred_element_type=jnp.f...  6.78 us
  transfers between devices with their start and end apart: 4, of which 3 were waited for; matrix products, arithmetic and copies ran while one was open for 17% of the time, Pallas kernels for 0%

commit v1 on v0

v1 whole, which is shorter than its diff:
```python
import functools

import jax
import jax.numpy as jnp
from jax import lax
from jax.experimental import pallas as pl
from jax.experimental.pallas import tpu as pltpu
from jax.sharding import PartitionSpec as P

AD_DEV = 8
RANK = 64
CORES = 2
CHUNKS = 4
PIECES = 2
AHEAD = 3
MESH = pl.DeviceIdType.MESH
BF16 = jnp.bfloat16
F32 = jnp.float32


def kernel(
    G, A, N, C, Q, T,
    tok_h, w_h, down_h, up_h, idx_ref, out_h,
    tok, w, down, up, part, in_r, in_l, idx_col, acc, mine, s_r, s_l, f_r, f_l, total, delta, result,
    load_tok, load_w, load_own, store_out,
    zs_r, zr_r, zs_l, zr_l, ss, sr, ys, yr, xs, xr, os, orr, cs, cr,
):
    Y = A // CORES
    K = (N - 1) * C
    g, a, z = lax.axis_index("groups"), lax.axis_index("adapter"), lax.axis_index("tensor")
    y, core = a // CORES, a % CORES
    R, KD = tok.shape[1], tok.shape[2]
    NB = w.shape[2]
    WD = down.shape[2]
    U = up.shape[1]
    flip = z // (N // 2)

    def block_at(j):
        return (N - 1 - j) * (1 - flip) + j * flip

    def tok_copy(c):
        return pltpu.make_async_copy(tok_h.at[pl.ds(c * R, R)], tok.at[c], load_tok.at[c])

    def w_copy(b):
        columns = pl.ds(pl.multiple_of(b * NB, NB), NB)
        return pltpu.make_async_copy(w_h.at[:, columns], w.at[b], load_w.at[b])

    own_copies = [
        pltpu.make_async_copy(down_h, down.at[a], load_own.at[0]),
        pltpu.make_async_copy(up_h, up.at[a], load_own.at[1]),
    ]
    tok_copy(0).start()
    w_copy(block_at(0)).start()
    for copy in own_copies:
        copy.start()
    for c in range(1, C):
        tok_copy(c).start()
    for j in range(1, N):
        w_copy(block_at(j)).start()

    z_right, z_left = (z + 1) % N, (z + N - 1) % N
    y_next, y_before = ((y + 1) % Y) * CORES + core, ((y + Y - 1) % Y) * CORES + core
    sibling = y * CORES + (CORES - 1 - core)
    greeted = [(g, a, z_right), (g, a, z_left), (g, y_next, z), (g, y_before, z), (g, sibling, z)]
    greeted += [((g + d) % G, a, z) for d in range(1, G)]
    barrier = pltpu.get_barrier_semaphore()
    for device in greeted:
        pl.semaphore_signal(barrier, inc=1, device_id=device, device_id_type=MESH)
    pl.semaphore_wait(barrier, len(greeted))

    def remote(src, dst, send, recv, device):
        return pltpu.make_async_remote_copy(
            src_ref=src, dst_ref=dst, send_sem=send, recv_sem=recv,
            device_id=device, device_id_type=MESH,
        )

    def piece(blk, share, i):
        if i < Q:
            rows = KD // G // Q
            first = pl.multiple_of(share * (KD // G) + i * rows, rows)
            return down.at[blk, pl.ds(first, rows)]
        rows = U // G
        return up.at[blk, pl.ds(pl.multiple_of(share * rows, rows), rows)]

    def y_copy(s, i):
        ref = piece(((y - s + Y) % Y) * CORES + core, g, i)
        return remote(ref, ref, ys.at[s, i], yr.at[s, i], (g, y_next, z))

    def y_landed(s, i):
        ref = piece(((y - s - 1 + Y) % Y) * CORES + core, g, i)
        return remote(ref, ref, ys.at[s, i], yr.at[s, i], (g, y_next, z))

    def x_copy(s, d, i):
        ref = piece(((y - s - 1 + Y) % Y) * CORES + core, g, i)
        return remote(ref, ref, xs.at[s, d - 1, i], xr.at[s, d - 1, i], ((g + d) % G, a, z))

    def x_landed(s, d, i):
        ref = piece(((y - s - 1 + Y) % Y) * CORES + core, (g - d + G) % G, i)
        return remote(ref, ref, xs.at[s, d - 1, i], xr.at[s, d - 1, i], ((g + d) % G, a, z))

    def core_copy(s, d, i, owner):
        ref = piece(((y - s - 1 + Y) % Y) * CORES + owner, (g - d + G) % G, i)
        return remote(ref, ref, cs.at[s, d, i], cr.at[s, d, i], (g, sibling, z))

    def own_copy(i, blk):
        ref = (down if i == 0 else up).at[blk]
        return remote(ref, ref, os.at[i], orr.at[i], (g, sibling, z))

    for i, copy in enumerate(own_copies):
        copy.wait()
        for q in (range(Q) if i == 0 else [Q]):
            y_copy(0, q).start()
        own_copy(i, a).start()

    def send_r(k, src):
        return remote(src, in_r.at[k], zs_r.at[k], zr_r.at[k], (g, a, z_right))

    def send_l(k, src):
        return remote(src, in_l.at[k], zs_l.at[k], zr_l.at[k], (g, a, z_left))

    def product(t, carry):
        j, c = t // C, t % C
        b = block_at(j)

        @pl.when(j == 0)
        def _():
            tok_copy(c).wait()

        @pl.when(c == 0)
        def _():
            w_copy(b).wait()

        part[b, c] = jnp.dot(tok[c], w[b], preferred_element_type=F32).astype(BF16)

        @pl.when((z == 0) & (t < T))
        def _():
            send_r(t, part.at[b, c]).start()

        @pl.when((z == N - 1) & (t < T))
        def _():
            send_l(t, part.at[b, c]).start()

        return carry

    lax.fori_loop(0, N * C, product, 0)

    turned = idx_ref[...].T
    groups_of_rows = idx_ref.shape[0]
    for r in range(groups_of_rows):
        idx_col[pl.ds(r * 128, 128)] = jnp.broadcast_to(turned[:, r:r + 1], (128, 128))

    lane = lax.broadcasted_iota(jnp.int32, (R, 128), 1)
    low = lane < RANK
    half = lane // RANK

    def rows_of(c):
        return pl.ds(pl.multiple_of(c * R, R), R)

    def shrink(blk, first):
        def step(c, carry):
            product = jnp.dot(tok[c], down[blk], preferred_element_type=F32)
            adapter = idx_col[rows_of(c)] - blk * AD_DEV
            kept = jnp.zeros((R, 128), F32)
            for n in range(WD // 128):
                hit = adapter == half + 2 * n
                kept = kept + jnp.where(hit, product[:, n * 128:(n + 1) * 128], 0.0)
            acc[c] = kept if first else acc[c] + kept
            return carry

        lax.fori_loop(0, C, step, 0)

    def pack():
        for c in range(C // 2):
            top, bottom = acc[c], acc[c + C // 2]
            top = top + pltpu.roll(top, RANK, 1)
            bottom = bottom + pltpu.roll(bottom, RANK, 1)
            mine[c] = jnp.where(low, top, bottom).astype(BF16)

    def sum_r(src):
        return remote(src, s_r, ss.at[0], sr.at[0], (g, a, z_right))

    def sum_l(src):
        return remote(src, s_l, ss.at[1], sr.at[1], (g, a, z_left))

    def gather_tasks():
        tasks = []
        for s in range(Y - 1):
            order = [("y", 0), ("y", 1), ("y", 2), ("x", 0), ("x", 1), ("x", 2)]
            tasks += [(kind, s, i) for kind, i in order]
        return tasks

    def run_task(kind, s, i):
        if kind == "y":
            y_landed(s, i).wait_recv()
            if s < Y - 2:
                y_copy(s + 1, i).start()
            for d in range(1, G):
                x_copy(s, d, i).start()
            core_copy(s, 0, i, core).start()
        else:
            for d in range(1, G):
                x_landed(s, d, i).wait_recv()
                core_copy(s, d, i, core).start()

    last = 7 * C // 4
    tasks = gather_tasks()
    places = [1, 3, 4, 4, 5, 6]
    plan = {}
    for n, task in enumerate(tasks):
        at = places[n] * C // 4 if Y == 2 else last
        plan.setdefault(at, []).append(task)

    for k in range(K):
        b_r, b_l, c = N - 1 - k // C, k // C, k % C

        @pl.when(z == 0)
        def _():
            if k >= T:
                send_r(k - T, part.at[N - 1 - (k - T) // C, (k - T) % C]).wait_send()
                send_r(k, part.at[b_r, c]).start()

        @pl.when(z == N - 1)
        def _():
            if k >= T:
                send_l(k - T, part.at[(k - T) // C, (k - T) % C]).wait_send()
                send_l(k, part.at[b_l, c]).start()

        @pl.when((z > 0) & (z < b_r))
        def _():
            send_r(k, in_r.at[k]).wait_recv()
            in_r[k] = (in_r[k].astype(F32) + part[b_r, c].astype(F32)).astype(BF16)
            send_r(k, in_r.at[k]).start()

        @pl.when((z < N - 1) & (z > b_l))
        def _():
            send_l(k, in_l.at[k]).wait_recv()
            in_l[k] = (in_l[k].astype(F32) + part[b_l, c].astype(F32)).astype(BF16)
            send_l(k, in_l.at[k]).start()

        for task in plan.get(k, []):
            run_task(*task)
        if k == C // 4:
            shrink(a, True)
        if k == 2 * C // 4:
            own_copy(0, sibling).wait_recv()
            own_copy(1, sibling).wait_recv()
            shrink(sibling, False)
        if k == last:
            for s in range(Y - 1):
                shrink(((y - s - 1 + Y) % Y) * CORES + core, False)
            for s in range(Y - 1):
                for d in range(G):
                    for i in range(Q + 1):
                        core_copy(s, d, i, CORES - 1 - core).wait_recv()
                shrink(((y - s - 1 + Y) % Y) * CORES + CORES - 1 - core, False)
            pack()

            @pl.when(z == 0)
            def _():
                sum_r(mine).start()

            @pl.when(z == N - 1)
            def _():
                sum_l(mine).start()

    total[...] = mine[...].astype(F32)

    def chain_r():
        @pl.when(z > 0)
        def _():
            sum_r(s_r).wait_recv()
            total[...] += s_r[...].astype(F32)

        @pl.when((z > 0) & (z < N - 1))
        def _():
            f_r[...] = (s_r[...].astype(F32) + mine[...].astype(F32)).astype(BF16)
            sum_r(f_r).start()

    def chain_l():
        @pl.when(z < N - 1)
        def _():
            sum_l(s_l).wait_recv()
            total[...] += s_l[...].astype(F32)

        @pl.when((z > 0) & (z < N - 1))
        def _():
            f_l[...] = (s_l[...].astype(F32) + mine[...].astype(F32)).astype(BF16)
            sum_l(f_l).start()

    @pl.when(flip == 0)
    def _():
        chain_r()
        chain_l()

    @pl.when(flip == 1)
    def _():
        chain_l()
        chain_r()

    def expand(c, carry):
        packed = total[c % (C // 2)]
        rolled = pltpu.roll(packed, RANK, 1)
        upper = (c // (C // 2)) == 0
        keep = low == upper
        both = jnp.where(keep, packed, rolled)
        adapter = idx_col[rows_of(c)]
        sums = jnp.zeros((R, NB), F32)
        for blk in range(A):
            wide = [
                jnp.where(adapter == half + (blk * AD_DEV + 2 * n), both, 0.0).astype(BF16)
                for n in range(U // 128)
            ]
            sums = sums + jnp.dot(
                jnp.concatenate(wide, axis=1), up[blk], preferred_element_type=F32
            )
        delta[c] = sums.astype(BF16)
        return carry

    lax.fori_loop(0, C, expand, 0)

    def out_copy(c):
        return pltpu.make_async_copy(result.at[c], out_h.at[rows_of(c)], store_out.at[c])

    def finish(c, carry):
        k_r, k_l = (N - 1 - z) * C + c, z * C + c

        @pl.when(z == 0)
        def _():
            send_l(k_l, in_l.at[k_l]).wait_recv()
            result[c] = (
                part[z, c].astype(F32) + in_l[k_l].astype(F32) + delta[c].astype(F32)
            ).astype(BF16)

        @pl.when(z == N - 1)
        def _():
            send_r(k_r, in_r.at[k_r]).wait_recv()
            result[c] = (
                part[z, c].astype(F32) + in_r[k_r].astype(F32) + delta[c].astype(F32)
            ).astype(BF16)

        @pl.when((z > 0) & (z < N - 1))
        def _():
            send_l(k_l, in_l.at[k_l]).wait_recv()
            send_r(k_r, in_r.at[k_r]).wait_recv()
            result[c] = (
                part[z, c].astype(F32)
                + in_r[k_r].astype(F32)
                + in_l[k_l].astype(F32)
                + delta[c].astype(F32)
            ).astype(BF16)

        out_copy(c).start()
        return carry

    lax.fori_loop(0, C, finish, 0)

    for k in range(K):
        b_r, b_l = N - 1 - k // C, k // C

        if k >= K - T:
            @pl.when(z == 0)
            def _():
                send_r(k, part.at[b_r, k % C]).wait_send()

            @pl.when(z == N - 1)
            def _():
                send_l(k, part.at[b_l, k % C]).wait_send()

        @pl.when((z > 0) & (z < b_r))
        def _():
            send_r(k, in_r.at[k]).wait_send()

        @pl.when((z < N - 1) & (z > b_l))
        def _():
            send_l(k, in_l.at[k]).wait_send()

    @pl.when(z < N - 1)
    def _():
        sum_r(f_r).wait_send()

    @pl.when(z > 0)
    def _():
        sum_l(f_l).wait_send()

    for i in range(2):
        own_copy(i, a).wait_send()
    for s in range(Y - 1):
        for i in range(Q + 1):
            y_copy(s, i).wait_send()
            for d in range(1, G):
                x_copy(s, d, i).wait_send()
            for d in range(G):
                core_copy(s, d, i, core).wait_send()
    for c in range(C):
        out_copy(c).wait()


def per_device(G, A, N, tokens, shared_weight, adapter_down_weight, adapter_up_weight, row_adapter_index):
    rows, depth = tokens.shape
    C, Q, T = CHUNKS, PIECES, AHEAD
    R = rows // C
    NB = shared_weight.shape[1] // N
    WD = adapter_down_weight.shape[1]
    U = adapter_up_weight.shape[0]
    K = (N - 1) * C
    Y = A // CORES
    DMA = pltpu.SemaphoreType.DMA
    hbm = pl.BlockSpec(memory_space=pl.ANY)
    return pl.pallas_call(
        functools.partial(kernel, G, A, N, C, Q, T),
        out_shape=jax.ShapeDtypeStruct((rows, NB), BF16),
        in_specs=[hbm] * 4 + [pl.BlockSpec(memory_space=pltpu.VMEM)],
        out_specs=hbm,
        scratch_shapes=[
            pltpu.VMEM((C, R, depth), BF16),
            pltpu.VMEM((N, depth, NB), BF16),
            pltpu.VMEM((A, depth, WD), BF16),
            pltpu.VMEM((A, U, NB), BF16),
            pltpu.VMEM((N, C, R, NB), BF16),
            pltpu.VMEM((K, R, NB), BF16),
            pltpu.VMEM((K, R, NB), BF16),
            pltpu.VMEM((rows, 128), jnp.int32),
            pltpu.VMEM((C, R, 128), F32),
            pltpu.VMEM((C // 2, R, 128), BF16),
            pltpu.VMEM((C // 2, R, 128), BF16),
            pltpu.VMEM((C // 2, R, 128), BF16),
            pltpu.VMEM((C // 2, R, 128), BF16),
            pltpu.VMEM((C // 2, R, 128), BF16),
            pltpu.VMEM((C // 2, R, 128), F32),
            pltpu.VMEM((C, R, NB), BF16),
            pltpu.VMEM((C, R, NB), BF16),
            DMA((C,)), DMA((N,)), DMA((2,)), DMA((C,)),
            DMA((K,)), DMA((K,)), DMA((K,)), DMA((K,)),
            DMA((2,)), DMA((2,)),
            DMA((Y - 1, Q + 1)), DMA((Y - 1, Q + 1)),
            DMA((Y - 1, G - 1, Q + 1)), DMA((Y - 1, G - 1, Q + 1)),
            DMA((2,)), DMA((2,)),
            DMA((Y - 1, G, Q + 1)), DMA((Y - 1, G, Q + 1)),
        ],
        compiler_params=pltpu.CompilerParams(
            collective_id=0, has_side_effects=True, vmem_limit_bytes=56 * 2**20
        ),
        cost_estimate=pl.CostEstimate(
            flops=4 * rows * depth * NB * N, bytes_accessed=16 * 2**20, transcendentals=0
        ),
    )(tokens, shared_weight, adapter_down_weight, adapter_up_weight,
      row_adapter_index.reshape(rows // 128, 128))


def solution(mesh):
    in_specs = (
        P(("groups", "adapter"), "tensor"),
        P("tensor", None),
        P("tensor", "adapter"),
        P("adapter", "tensor"),
        P(("groups", "adapter")),
    )
    out_specs = P(("groups", "adapter"), "tensor")
    shape = mesh.shape
    body = functools.partial(per_device, shape["groups"], shape["adapter"], shape["tensor"])
    return jax.shard_map(
        body, mesh=mesh, in_specs=in_specs, out_specs=out_specs, check_vma=False
    )
```

time: 235 us -> 108 us (0.46)
  waiting for transfers between devices: 131 us -> 0 us
  Pallas kernels: 0 us -> 105 us
  local copies, waits for them, and re-layouts: 32.1 us -> 2.26 us
  matrix products: 21.5 us -> 0 us
  blocking collectives: 19.8 us -> 0 us
  between operations: 13.5 us -> 0.01 us
  starting transfers between devices: 9.71 us -> 0 us
  other arithmetic: 6.4 us -> 0 us
    pallas_call x0 -> x1, Pallas kernels: none -> 105 us  [per_device(): pl.pallas_call(functools.partial(kernel, G, A, N, C, Q, T), out_shape=jax...]
    all_to_all x2 -> x0, waiting for transfers between devices: 56.6 us -> none  [the longest x1 56.6 us: foreign_rows(): lax.all_to_all(gathered_rows, 'adapter', split_axis=0, concat_axis=0, til...]
    reduce_scatter x1 -> x0, waiting for transfers between devices: 53.1 us -> none  [per_device(): lax.psum_scatter(base_partial.astype(jnp.bfloat16), 'tensor', scatter_dim...]
    psum x1 -> x0, waiting for transfers between devices: 21.7 us -> none  [foreign_rows(): reduced_rows = lax.psum(partial_value.astype(jnp.bfloat16), 'tensor')]
    dot_general x3 -> x0, matrix products: 21.5 us -> none  [the longest x1 13.8 us: per_device(): jnp.dot(tokens, shared_weight, preferred_element_type=jnp.float32)]
    all_to_all x1 -> x0, blocking collectives: 19.8 us -> none  [foreign_rows(): lax.all_to_all(delta_rows, 'adapter', split_axis=0, concat_axis=0, tiled=...]
    scatter x2 -> x0, local copies, waits for them, and re-layouts: 18.3 us -> none  [the longest x1 10.7 us: pack_rows(): jnp.zeros((holders * capacity + 1, width), jnp.bfloat16).at[slot_index]]
    all_to_all x2 -> x0, starting transfers between devices: 9.44 us -> none  [the longest x1 5.21 us: foreign_rows(): lax.all_to_all(gathered_rows, 'adapter', split_axis=0, concat_axis=0, til...]
  transfers between devices with their start and end apart: 4 -> 0, of which waited for: 3 -> 0; matrix products, arithmetic and copies ran while one was open for 17% -> 0% of each run, Pallas kernels for 0% -> 0%
where the time goes in v1:
time: 108 us; the launch traced here: 107 us
  Pallas kernels  105 us (97%)
  local copies, waits for them, and re-layouts  2.26 us (2%)
    pallas_call x1, Pallas kernels, per_device(): pl.pallas_call(functools.partial(kernel, G, A, N, C, Q, T), out_shape=jax...  105 us
    unnamed x1, local copies, waits for them, and re-layouts  2.26 us

profile of v1, /device:TPU:0, one launch (start us, length us, event | category | flops | bytes accessed | tf_op | source)
XLA Modules:
  0.0 107.5 jit_solution(14614382727098089535)
XLA Ops:
  0.0 105.2 %shard_map.55 = bf16[1024,512]{1,0:T(8,128)(2,1)} custom-call(bf16[1024,2048]{1,0:T(8,128)(2,1)} %tok_h.1, bf16[2048,2048]{1,0:T(8,128)(2,1)} %w_h.1, bf16[2048,512]{1,0:T(8,128)(2,1)} %down_h.1, bf16[512,512]{1,0:T(8,128)(2,1)} %up_h.1, s32[8,128]{1,0:T(8,128)} %bitcast.1), custom_call_target="tpu_custom_call" | custom-call | flops 17179869184 | bytes 16777216 | tf_op jit(solution)/shard_map/pallas_call | solution.py:409
  105.2 2.3 %copy.7 = bf16[1024,512]{1,0:T(8,128)(2,1)} copy(bf16[1024,512]{1,0:T(8,128)(2,1)} %shard_map.55) | data formatting | bytes 2097152

commit v2 on v1

--- a/solution.py
+++ b/solution.py
@@ -10,9 +10,11 @@
 AD_DEV = 8
 RANK = 64
 CORES = 2
-CHUNKS = 4
-PIECES = 2
-AHEAD = 3
+CHUNKS = 8
+TILES = 2
+PIECES = 4
+AHEAD = 4
+LAG = 2
 MESH = pl.DeviceIdType.MESH
 BF16 = jnp.bfloat16
 F32 = jnp.float32
@@ -29,7 +31,10 @@
     K = (N - 1) * C
     g, a, z = lax.axis_index("groups"), lax.axis_index("adapter"), lax.axis_index("tensor")
     y, core = a // CORES, a % CORES
-    R, KD = tok.shape[1], tok.shape[2]
+    M, KD = tok.shape[1], tok.shape[2]
+    R = part.shape[2]
+    B = tok.shape[0]
+    S = C // B
     NB = w.shape[2]
     WD = down.shape[2]
     U = up.shape[1]
@@ -39,7 +44,7 @@
         return (N - 1 - j) * (1 - flip) + j * flip
 
     def tok_copy(c):
-        return pltpu.make_async_copy(tok_h.at[pl.ds(c * R, R)], tok.at[c], load_tok.at[c])
+        return pltpu.make_async_copy(tok_h.at[pl.ds(c * M, M)], tok.at[c], load_tok.at[c])
 
     def w_copy(b):
         columns = pl.ds(pl.multiple_of(b * NB, NB), NB)
@@ -53,7 +58,7 @@
     w_copy(block_at(0)).start()
     for copy in own_copies:
         copy.start()
-    for c in range(1, C):
+    for c in range(1, B):
         tok_copy(c).start()
     for j in range(1, N):
         w_copy(block_at(j)).start()
@@ -119,59 +124,67 @@
         return remote(src, in_l.at[k], zs_l.at[k], zr_l.at[k], (g, a, z_left))
 
     def product(t, carry):
-        j, c = t // C, t % C
+        j, m = t // B, t % B
         b = block_at(j)
 
         @pl.when(j == 0)
         def _():
-            tok_copy(c).wait()
-
-        @pl.when(c == 0)
+            tok_copy(m).wait()
+
+        @pl.when(m == 0)
         def _():
             w_copy(b).wait()
 
-        part[b, c] = jnp.dot(tok[c], w[b], preferred_element_type=F32).astype(BF16)
-
-        @pl.when((z == 0) & (t < T))
-        def _():
-            send_r(t, part.at[b, c]).start()
-
-        @pl.when((z == N - 1) & (t < T))
-        def _():
-            send_l(t, part.at[b, c]).start()
+        dense = jnp.dot(tok[m], w[b], preferred_element_type=F32).astype(BF16)
+        for i in range(S):
+            part[b, m * S + i] = dense[i * R:(i + 1) * R]
+
+        for i in range(S):
+            k = t * S + i
+
+            @pl.when((z == 0) & (k < T))
+            def _():
+                send_r(k, part.at[b, m * S + i]).start()
+
+            @pl.when((z == N - 1) & (k < T))
+            def _():
+                send_l(k, part.at[b, m * S + i]).start()
 
         return carry
 
-    lax.fori_loop(0, N * C, product, 0)
+    lax.fori_loop(0, N * B, product, 0)
 
     turned = idx_ref[...].T
     groups_of_rows = idx_ref.shape[0]
     for r in range(groups_of_rows):
         idx_col[pl.ds(r * 128, 128)] = jnp.broadcast_to(turned[:, r:r + 1], (128, 128))
 
-    lane = lax.broadcasted_iota(jnp.int32, (R, 128), 1)
+    lane = lax.broadcasted_iota(jnp.int32, (M, 128), 1)
     low = lane < RANK
     half = lane // RANK
 
     def rows_of(c):
         return pl.ds(pl.multiple_of(c * R, R), R)
 
+    def rows_of_tile(m):
+        return pl.ds(pl.multiple_of(m * M, M), M)
+
     def shrink(blk, first):
-        def step(c, carry):
-            product = jnp.dot(tok[c], down[blk], preferred_element_type=F32)
-            adapter = idx_col[rows_of(c)] - blk * AD_DEV
-            kept = jnp.zeros((R, 128), F32)
+        def step(m, carry):
+            product = jnp.dot(tok[m], down[blk], preferred_element_type=F32)
+            adapter = idx_col[rows_of_tile(m)] - blk * AD_DEV
+            kept = jnp.zeros((M, 128), F32)
             for n in range(WD // 128):
                 hit = adapter == half + 2 * n
                 kept = kept + jnp.where(hit, product[:, n * 128:(n + 1) * 128], 0.0)
-            acc[c] = kept if first else acc[c] + kept
+            acc[m] = kept if first else acc[m] + kept
             return carry
 
-        lax.fori_loop(0, C, step, 0)
+        lax.fori_loop(0, B, step, 0)
 
     def pack():
-        for c in range(C // 2):
-            top, bottom = acc[c], acc[c + C // 2]
+        for c in range(B // 2):
+            top, bottom = acc[c], acc[c + B // 2]
             top = top + pltpu.roll(top, RANK, 1)
             bottom = bottom + pltpu.roll(bottom, RANK, 1)
             mine[c] = jnp.where(low, top, bottom).astype(BF16)
@@ -181,13 +194,6 @@
 
     def sum_l(src):
         return remote(src, s_l, ss.at[1], sr.at[1], (g, a, z_left))
-
-    def gather_tasks():
-        tasks = []
-        for s in range(Y - 1):
-            order = [("y", 0), ("y", 1), ("y", 2), ("x", 0), ("x", 1), ("x", 2)]
-            tasks += [(kind, s, i) for kind, i in order]
-        return tasks
 
     def run_task(kind, s, i):
         if kind == "y":
@@ -202,13 +208,37 @@
                 x_landed(s, d, i).wait_recv()
                 core_copy(s, d, i, core).start()
 
-    last = 7 * C // 4
-    tasks = gather_tasks()
-    places = [1, 3, 4, 4, 5, 6]
-    plan = {}
-    for n, task in enumerate(tasks):
-        at = places[n] * C // 4 if Y == 2 else last
-        plan.setdefault(at, []).append(task)
+    last = min(2 * C, K - 1)
+    order = []
+    for s in range(Y - 1):
+        order += [("y", s, 0)]
+        for i in range(1, Q + 1):
+            order += [("y", s, i), ("x", s, i - 1)]
+        order += [("x", s, Q)]
+    plan_end, plan_middle = {}, {}
+    for n, task in enumerate(order):
+        i = task[2] + (1 if task[0] == "x" else 0)
+        for plan, first in ((plan_end, T), (plan_middle, 0)):
+            at = min(first + 2 * i + 1, last) if Y == 2 else last
+            plan.setdefault(at, []).append(task)
+
+    def forward_r(k):
+        b_r, c = N - 1 - k // C, k % C
+
+        @pl.when((z > 0) & (z < b_r))
+        def _():
+            send_r(k, in_r.at[k]).wait_recv()
+            in_r[k] = (in_r[k].astype(F32) + part[b_r, c].astype(F32)).astype(BF16)
+            send_r(k, in_r.at[k]).start()
+
+    def forward_l(k):
+        b_l, c = k // C, k % C
+
+        @pl.when((z < N - 1) & (z > b_l))
+        def _():
+            send_l(k, in_l.at[k]).wait_recv()
+            in_l[k] = (in_l[k].astype(F32) + part[b_l, c].astype(F32)).astype(BF16)
+            send_l(k, in_l.at[k]).start()
 
     for k in range(K):
         b_r, b_l, c = N - 1 - k // C, k // C, k % C
@@ -225,23 +255,33 @@
                 send_l(k - T, part.at[(k - T) // C, (k - T) % C]).wait_send()
                 send_l(k, part.at[b_l, c]).start()
 
-        @pl.when((z > 0) & (z < b_r))
-        def _():
-            send_r(k, in_r.at[k]).wait_recv()
-            in_r[k] = (in_r[k].astype(F32) + part[b_r, c].astype(F32)).astype(BF16)
-            send_r(k, in_r.at[k]).start()
-
-        @pl.when((z < N - 1) & (z > b_l))
-        def _():
-            send_l(k, in_l.at[k]).wait_recv()
-            in_l[k] = (in_l[k].astype(F32) + part[b_l, c].astype(F32)).astype(BF16)
-            send_l(k, in_l.at[k]).start()
-
-        for task in plan.get(k, []):
-            run_task(*task)
-        if k == C // 4:
+        @pl.when(flip == 0)
+        def _():
+            forward_r(k)
+            if k >= LAG:
+                forward_l(k - LAG)
+
+        @pl.when(flip == 1)
+        def _():
+            forward_l(k)
+            if k >= LAG:
+                forward_r(k - LAG)
+
+        if k in plan_end:
+            @pl.when((z == 0) | (z == N - 1))
+            def _():
+                for task in plan_end[k]:
+                    run_task(*task)
+
+        if k in plan_middle:
+            @pl.when((z > 0) & (z < N - 1))
+            def _():
+                for task in plan_middle[k]:
+                    run_task(*task)
+
+        if k == C // 2:
             shrink(a, True)
-        if k == 2 * C // 4:
+        if k == 3 * C // 4:
             own_copy(0, sibling).wait_recv()
             own_copy(1, sibling).wait_recv()
             shrink(sibling, False)
@@ -297,14 +337,14 @@
         chain_l()
         chain_r()
 
-    def expand(c, carry):
-        packed = total[c % (C // 2)]
+    def expand(m, carry):
+        packed = total[m % (B // 2)]
         rolled = pltpu.roll(packed, RANK, 1)
-        upper = (c // (C // 2)) == 0
+        upper = (m // (B // 2)) == 0
         keep = low == upper
         both = jnp.where(keep, packed, rolled)
-        adapter = idx_col[rows_of(c)]
-        sums = jnp.zeros((R, NB), F32)
+        adapter = idx_col[rows_of_tile(m)]
+        sums = jnp.zeros((M, NB), F32)
         for blk in range(A):
             wide = [
                 jnp.where(adapter == half + (blk * AD_DEV + 2 * n), both, 0.0).astype(BF16)
@@ -313,10 +353,12 @@
             sums = sums + jnp.dot(
                 jnp.concatenate(wide, axis=1), up[blk], preferred_element_type=F32
             )
-        delta[c] = sums.astype(BF16)
+        sums = sums.astype(BF16)
+        for i in range(S):
+            delta[m * S + i] = sums[i * R:(i + 1) * R]
         return carry
 
-    lax.fori_loop(0, C, expand, 0)
+    lax.fori_loop(0, B, expand, 0)
 
     def out_copy(c):
         return pltpu.make_async_copy(result.at[c], out_h.at[rows_of(c)], store_out.at[c])
@@ -397,8 +439,8 @@
 
 def per_device(G, A, N, tokens, shared_weight, adapter_down_weight, adapter_up_weight, row_adapter_index):
     rows, depth = tokens.shape
-    C, Q, T = CHUNKS, PIECES, AHEAD
-    R = rows // C
+    C, B, Q, T = CHUNKS, TILES, PIECES, AHEAD
+    R, M = rows // C, rows // B
     NB = shared_weight.shape[1] // N
     WD = adapter_down_weight.shape[1]
     U = adapter_up_weight.shape[0]
@@ -412,7 +454,7 @@
         in_specs=[hbm] * 4 + [pl.BlockSpec(memory_space=pltpu.VMEM)],
         out_specs=hbm,
         scratch_shapes=[
-            pltpu.VMEM((C, R, depth), BF16),
+            pltpu.VMEM((B, M, depth), BF16),
             pltpu.VMEM((N, depth, NB), BF16),
             pltpu.VMEM((A, depth, WD), BF16),
             pltpu.VMEM((A, U, NB), BF16),
@@ -420,16 +462,16 @@
             pltpu.VMEM((K, R, NB), BF16),
             pltpu.VMEM((K, R, NB), BF16),
             pltpu.VMEM((rows, 128), jnp.int32),
-            pltpu.VMEM((C, R, 128), F32),
-            pltpu.VMEM((C // 2, R, 128), BF16),
-            pltpu.VMEM((C // 2, R, 128), BF16),
-            pltpu.VMEM((C // 2, R, 128), BF16),
-            pltpu.VMEM((C // 2, R, 128), BF16),
-            pltpu.VMEM((C // 2, R, 128), BF16),
-            pltpu.VMEM((C // 2, R, 128), F32),
+            pltpu.VMEM((B, M, 128), F32),
+            pltpu.VMEM((B // 2, M, 128), BF16),
+            pltpu.VMEM((B // 2, M, 128), BF16),
+            pltpu.VMEM((B // 2, M, 128), BF16),
+            pltpu.VMEM((B // 2, M, 128), BF16),
+            pltpu.VMEM((B // 2, M, 128), BF16),
+            pltpu.VMEM((B // 2, M, 128), F32),
             pltpu.VMEM((C, R, NB), BF16),
             pltpu.VMEM((C, R, NB), BF16),
-            DMA((C,)), DMA((N,)), DMA((2,)), DMA((C,)),
+            DMA((B,)), DMA((N,)), DMA((2,)), DMA((C,)),
             DMA((K,)), DMA((K,)), DMA((K,)), DMA((K,)),
             DMA((2,)), DMA((2,)),
             DMA((Y - 1, Q + 1)), DMA((Y - 1, Q + 1)),

time: 108 us -> 83.2 us (0.77)
  the two profiles are of different devices: /device:TPU:0 before, /device:TPU:16 now
where the time goes in v2:
time: 83.2 us; the launch traced here: 83 us
  Pallas kernels  80.7 us (97%)
  local copies, waits for them, and re-layouts  2.26 us (3%)
    pallas_call x1, Pallas kernels, per_device(): pl.pallas_call(functools.partial(kernel, G, A, N, C, Q, T), out_shape=jax...  80.7 us
    unnamed x1, local copies, waits for them, and re-layouts  2.26 us

profile of v2, /device:TPU:16, one launch (start us, length us, event | category | flops | bytes accessed | tf_op | source)
XLA Modules:
  0.0 83.0 jit_solution(14746975980999097283)
XLA Ops:
  0.0 80.7 %shard_map.55 = bf16[1024,512]{1,0:T(8,128)(2,1)} custom-call(bf16[1024,2048]{1,0:T(8,128)(2,1)} %tok_h.1, bf16[2048,2048]{1,0:T(8,128)(2,1)} %w_h.1, bf16[2048,512]{1,0:T(8,128)(2,1)} %down_h.1, bf16[512,512]{1,0:T(8,128)(2,1)} %up_h.1, s32[8,128]{1,0:T(8,128)} %bitcast.1), custom_call_target="tpu_custom_call" | custom-call | flops 17179869184 | bytes 16777216 | tf_op jit(solution)/shard_map/pallas_call | solution.py:451
  80.7 2.3 %copy.7 = bf16[1024,512]{1,0:T(8,128)(2,1)} copy(bf16[1024,512]{1,0:T(8,128)(2,1)} %shard_map.55) | data formatting | bytes 2097152
